TPU v7x, 512 devices: a whole 4x4x16 slice. The times are simulated.
512 devices in a mesh: seq: 32 (over x, y, core), exp: 16 (over z).
Axes of the slice: x: 4, y: 4, z: 16, core: 2. Of those that a mesh axis runs over, the one named last changes fastest.
Arguments:
- tokens: bfloat16 [65536, 1024], P('seq', 'exp'), may hold values from -12 to 12
- routing: bfloat16 [1024, 2048], P(None, 'exp'), may hold values from -2 to 2
- w_in: bfloat16 [128, 1024, 4096], P('exp', None, 'seq'), may hold values from -0.1875 to 0.1875
- w_out: bfloat16 [128, 4096, 1024], P('exp', 'seq'), may hold values from -0.09375 to 0.09375
Outputs:
- mixed_tokens: bfloat16 [65536, 1024], P('seq', 'exp')
All inputs are finite; a program needn't handle non-finite values.
Results may differ from a plain program's by a relative error of at most 0.02.
Values may be sent and summed in bfloat16 or wider, within the bound.
A program may use at most 128 MiB of HBM per device.

v0:
```python
import jax
import jax.numpy as jnp
from jax import lax
from jax.sharding import PartitionSpec as P


def shards(tokens, routing, w_in, w_out):
    features = lax.all_gather(tokens, "exp", axis=1, tiled=True)
    logits = jnp.dot(features, routing, preferred_element_type=jnp.float32)
    local_peak = jnp.max(logits, axis=0)
    exponent = jnp.exp(logits - local_peak)
    local_total = jnp.sum(exponent, axis=0)
    local_rows = lax.dot_general(
        exponent.astype(jnp.bfloat16),
        features,
        (((0,), (0,)), ((), ())),
        preferred_element_type=jnp.float32,
    )
    slot_peak = lax.pmax(local_peak, "seq")
    factor = jnp.exp(local_peak - slot_peak)
    slot_total, slot_rows = lax.psum((local_total * factor, local_rows * factor[:, None]), "seq")
    slot_inputs = (slot_rows / slot_total[:, None]).astype(jnp.bfloat16)
    width = slot_inputs.shape[1]
    grouped = slot_inputs.reshape(w_in.shape[0], -1, width)
    hidden = jax.nn.gelu(
        jnp.einsum("esd,edh->esh", grouped, w_in, preferred_element_type=jnp.float32),
        approximate=True,
    ).astype(jnp.bfloat16)
    partial_out = jnp.einsum(
        "esh,ehd->esd", hidden, w_out, preferred_element_type=jnp.float32
    ).reshape(slot_inputs.shape)
    expert_out = lax.psum(partial_out, "seq").astype(jnp.bfloat16)
    row_peak = jnp.max(logits, axis=1)
    token_peak = lax.pmax(row_peak, "exp")
    combine_expo = jnp.exp(logits - token_peak[:, None])
    token_total = lax.psum(jnp.sum(combine_expo, axis=1), "exp")
    weights = combine_expo.astype(jnp.bfloat16)
    group_rows = (
        jnp.dot(weights, expert_out, preferred_element_type=jnp.float32)
        .astype(jnp.bfloat16)
        .astype(jnp.float32)
    )
    summed = lax.psum_scatter(
        group_rows.astype(jnp.bfloat16), "exp", scatter_dimension=1, tiled=True
    ).astype(jnp.float32)
    return (summed / token_total[:, None]).astype(jnp.bfloat16)


def solution(mesh):
    in_specs = (P("seq", "exp"), P(None, "exp"), P("exp", None, "seq"), P("exp", "seq", None))
    out_specs = P("seq", "exp")
    return jax.shard_map(shards, mesh=mesh, in_specs=in_specs, out_specs=out_specs, check_vma=False)
```

profile of v0, /device:TPU:30, one launch (start us, length us, event | category | flops | bytes accessed | tf_op | source)
XLA Modules:
  0.0 543.8 jit_solution(6115946723204241180)
XLA Ops:
  6.5 0.0 copy-start
  6.5 0.0 all-gather.2.cloned.1.call-start
  6.5 0.7 all-gather.2.cloned.1.call-update
  7.3 0.0 all-reduce.3.cloned.1.call-start
  7.3 85.1 %all-gather.2.cloned.1.call-done = bf16[2048,1024]{0,1:T(8,128)(2,1)} async-done(((bf16[2048,64]{0,1:T(8,128)(2,1)}), bf16[2048,1024]{0,1:T(8,128)(2,1)}) %all-gather.2.cloned.1.call-update) | async-done | bytes 4194320 | tf_op jit(solution)/shard_map/all_gather | solution.py:8
  92.5 3.7 fusion.27
  96.1 30.2 %pmax.14 = f32[2048]{0:T(1024)S(1)} all-reduce(f32[2048]{0:T(1024)S(1)} %get-tuple-element.8), channel_id=1, replica_groups=mesh['seq'=32,'exp'=16] {'exp'}, use_global_device_ids=true, to_apply=%region_1.0 | all-reduce | flops 2048 | bytes 16384 | tf_op jit(solution)/shard_map/pmax | solution.py:34
  126.3 57.1 %pmax.15 = f32[128]{0:T(128)S(1)} all-reduce(f32[128]{0:T(128)S(1)} %get-tuple-element.7), channel_id=1, replica_groups=mesh['seq'=32,'exp'=16] {'seq'}, use_global_device_ids=true, to_apply=%region_3.0 | all-reduce | flops 128 | bytes 1024 | tf_op jit(solution)/shard_map/pmax | solution.py:19
  183.4 0.6 fusion
  184.1 4.5 convolution_multiply_fusion
  188.6 0.0 all-reduce.3.cloned.1.call-update
  188.6 0.0 reduce-scatter.2.cloned.1.call-start
  188.7 62.7 %psum.29 = f32[128]{0:T(128)S(1)} all-reduce(f32[128]{0:T(128)S(1)} %get-tuple-element.9), channel_id=1, replica_groups=mesh['seq'=32,'exp'=16] {'seq'}, use_global_device_ids=true, to_apply=%region_6.0 | all-reduce | flops 128 | bytes 1024 | tf_op jit(solution)/shard_map/psum | solution.py:21
  251.3 66.3 %all-reduce.3.cloned.1.call-done = f32[128,1024]{1,0:T(8,128)} async-done(((f32[128,1024]{1,0:T(8,128)}), f32[128,1024]{1,0:T(8,128)}) %all-reduce.3.cloned.1.call-update) | async-done | bytes 524304 | tf_op jit(solution)/shard_map/psum | solution.py:21
  317.6 1.1 divide_convert_fusion.1
  318.8 0.0 copy-done
  318.8 3.1 fusion.17
  321.9 128.7 %all-reduce.4 = bf16[128,1024]{1,0:T(8,128)(2,1)S(1)} all-reduce(f32[128,1024]{1,0:T(8,128)} %bitcast.9), channel_id=1, replica_groups=mesh['seq'=32,'exp'=16] {'seq'}, use_global_device_ids=true, to_apply=%region_7.0 | all-reduce | flops 131072 | bytes 786432 | tf_op jit(solution)/shard_map/psum | solution.py:32
  450.5 3.3 convolution_convert_fusion
  453.8 0.0 reduce-scatter.2.cloned.1.call-update
  453.9 32.1 %psum.31 = f32[2048]{0:T(1024)S(1)} all-reduce(f32[2048]{0:T(1024)S(1)} %get-tuple-element.5), channel_id=1, replica_groups=mesh['seq'=32,'exp'=16] {'exp'}, use_global_device_ids=true, to_apply=%region_10.0 | all-reduce | flops 2048 | bytes 16384 | tf_op jit(solution)/shard_map/psum | solution.py:36
  486.0 49.6 %reduce-scatter.2.cloned.1.call-done = bf16[2048,64]{0,1:T(8,128)(2,1)} async-done(((bf16[2048,1024]{0,1:T(8,128)(2,1)}), bf16[2048,64]{0,1:T(8,128)(2,1)}) %reduce-scatter.2.cloned.1.call-update) | async-done | bytes 262160 | tf_op jit(solution)/shard_map/reduce_scatter | solution.py:43
  535.6 1.7 divide_convert_fusion
  (1 shorter events, 0.0 us)
Async XLA Ops:
  6.5 312.3 %copy-start = (bf16[8,128,1024]{2,1,0:T(8,128)(2,1)S(1)}, bf16[8,128,1024]{2,1,0:T(8,128)(2,1)}, u32[]{:S(2)}) copy-start(bf16[8,128,1024]{2,1,0:T(8,128)(2,1)} %param.7) | copy-start | bytes 6291460
  6.5 85.9 %all-gather.2.cloned.1.call-start = ((), (), s32[]{:S(2)}) async-start(), calls=%async_computation.1 | async-start | bytes 4456448 | tf_op jit(solution)/shard_map/all_gather | solution.py:8
  7.3 310.4 %all-reduce.3.cloned.1.call-start = ((), (), s32[]{:S(2)}) async-start(), calls=%async_computation.2 | async-start | bytes 1048576 | tf_op jit(solution)/shard_map/psum | solution.py:21
  188.6 347.0 %reduce-scatter.2.cloned.1.call-start = ((), (), s32[]{:S(2)}) async-start(), calls=%async_computation.3 | async-start | bytes 4456448 | tf_op jit(solution)/shard_map/reduce_scatter | solution.py:43
Sparse Core Ops, SparseCore 0:
  9.4 82.9 all-gather.1
  188.7 128.8 all-reduce.2
  454.0 81.5 reduce-scatter.1
where the time goes:
time: 545 us; the launch traced here: 544 us
  blocking collectives  311 us (57%)
  waiting for transfers between devices  202 us (37%)
  matrix products  14.6 us (3%)
  between operations  13.2 us (2%)
    psum x1, blocking collectives, shards(): expert_out = lax.psum(partial_out, 'seq').astype(jnp.bfloat16)  129 us
    all_gather x1, waiting for transfers between devices, shards(): features = lax.all_gather(tokens, 'exp', axis=1, tiled=True)  85.1 us
    psum x1, waiting for transfers between devices, shards(): lax.psum((local_total * factor, local_rows * factor[:, None]), 'seq')  66.3 us
    psum x1, blocking collectives, shards(): lax.psum((local_total * factor, local_rows * factor[:, None]), 'seq')  62.7 us
    pmax x1, blocking collectives, shards(): slot_peak = lax.pmax(local_peak, 'seq')  57.1 us
    reduce_scatter x1, waiting for transfers between devices, shards(): lax.psum_scatter(group_rows.astype(jnp.bfloat16), 'exp', scatter_dimensio...  49.6 us
    psum x1, blocking collectives, shards(): token_total = lax.psum(jnp.sum(combine_expo, axis=1), 'exp')  32.1 us
    pmax x1, blocking collectives, shards(): token_peak = lax.pmax(row_peak, 'exp')  30.2 us
  transfers between devices with their start and end apart: 3, of which 3 were waited for; matrix products, arithmetic and copies ran while one was open for 0% of the time, Pallas kernels for 0%

commit v1 on v0

v1 whole, which is shorter than its diff:
```python
import functools

import jax
import jax.numpy as jnp
from jax import lax
from jax.experimental import pallas as pl
from jax.experimental.pallas import tpu as pltpu
from jax.sharding import PartitionSpec as P

MESH = pl.DeviceIdType.MESH
F32, BF16 = jnp.float32, jnp.bfloat16
N = 4
CHIPS = N * N
ROWS = 64
HALF = ROWS // 2
TOK = 128
FSET = {1: (2, 1), -1: (-1, 0)}


def remote(src, dst, send, recv, seq, z):
    return pltpu.make_async_remote_copy(
        src_ref=src, dst_ref=dst, send_sem=send, recv_sem=recv, device_id=(seq, z), device_id_type=MESH
    )


def kernel(nz, tok_ref, route_ref, win_ref, wout_ref, out_ref, *scratch):
    (
        xt, gr, ge, lg, wt, cw, stok, s, rf, rn, rf2, rn2, fb, mx, mxr, tt, ttr, zs, zst, zb, si, sp, pacc,
        pt, pb, osend, orecv, oown, ofin, trow, trow_r, prow, win, wout,
        tok_s, tok_r, xs_s, xs_r, rz_s, rz_r, ag_s, ag_r, ae_s, ae_r, rs_s, rs_r, mx_s, mx_r, tt_s, tt_r, zs_s, zs_r,
        zb_s, zb_r, si_s, si_r, pt_s, pt_r, ez_s, ez_r, os_s, os_r, fin_s, fin_r, tr_s, tr_r, w_s, own_s,
    ) = scratch
    seq, z = lax.axis_index("seq"), lax.axis_index("exp")
    x, y, c = seq // (2 * N), (seq // 2) % N, seq % 2
    p = seq // 2
    planes = nz // 2
    width = 128 * planes
    feats = xt.shape[0]
    fz = feats // nz
    owner = c == z % 2
    oc = z % 2
    mine = pl.multiple_of((z // 2) * 128, 128)
    other = 2 * p + 1 - c

    def zpeer(k):
        return (z + k) % nz

    def chip(k):
        return (p + k) % CHIPS

    def lanes(j):
        return pl.ds(pl.multiple_of(j * 128, 128), 128)

    def rows(i, n):
        return pl.ds(pl.multiple_of(i * n, n), n)

    def loop(lo, hi):
        def run(body):
            def step(i, carry):
                body(i)
                return carry
            lax.fori_loop(lo, hi, step, 0)
        return run

    barrier = pltpu.get_barrier_semaphore()

    @loop(1, nz)
    def _(k):
        pl.semaphore_signal(barrier, inc=1, device_id=(seq, zpeer(k)), device_id_type=MESH)

    @loop(1, CHIPS)
    def _(k):
        pl.semaphore_signal(barrier, inc=1, device_id=(2 * chip(k) + c, z), device_id_type=MESH)
        pl.semaphore_signal(barrier, inc=1, device_id=(2 * chip(k) + 1 - c, z), device_id_type=MESH)

    pl.semaphore_signal(barrier, inc=1, device_id=(other, z), device_id_type=MESH)

    own_x = pltpu.make_async_copy(tok_ref.at[:, lanes(z)], xt.at[rows(z, fz), lanes(c)], own_s.at[0])
    own_x.start()
    own_r = pltpu.make_async_copy(route_ref.at[rows(p, ROWS), :], gr.at[x, y, :, pl.ds(mine, 128)], own_s.at[1])

    @pl.when(owner)
    def _():
        own_r.start()

    load_in = pltpu.make_async_copy(win_ref, win, w_s.at[0])
    load_out = pltpu.make_async_copy(wout_ref, wout, w_s.at[1])

    pl.semaphore_wait(barrier, nz - 1 + 2 * (CHIPS - 1) + 1)

    def rz_copy(k):
        return remote(
            route_ref.at[rows(p, ROWS), :], gr.at[x, y, :, pl.ds(mine, 128)], rz_s.at[k], rz_r.at[z // 2], seq, zpeer(k)
        )

    @pl.when(owner)
    def _():
        @loop(1, nz)
        def _(k):
            rz_copy(k).start()

    def tok_copy(k):
        to = zpeer(k)
        return remote(
            tok_ref.at[:, lanes(to)], xt.at[rows(z, fz), lanes(c)], tok_s.at[k], tok_r.at[z], seq, to
        )

    @loop(1, nz)
    def _(k):
        tok_copy(k).start()

    load_in.start()
    load_out.start()

    def near(h, axis, d):
        along_x = (axis == 1) == (h == 0)
        nx = (x + d) % N if along_x else x
        ny = y if along_x else (y + d) % N
        return 2 * (N * nx + ny) + c

    def place(h, o1, o2):
        return ((x + o1) % N, (y + o2) % N) if h == 0 else ((x + o2) % N, (y + o1) % N)

    def block(buf, h, o1, o2, lo=0, n=HALF):
        bx, by = place(h, o1, o2)
        return buf.at[bx, by, pl.ds(h * HALF + lo, n), :]

    OFF = (0, 1, -1, 2)
    QUART = HALF // 2

    def gather(buf, ss, rs):
        def s1(h, d):
            b = block(buf, h, 0, 0)
            i = 16 * h + (0 if d == 1 else 1)
            return remote(b, b, ss.at[i], rs.at[i], near(h, 1, d), z)

        def s1f(h, d):
            b = block(buf, h, -d, 0, 0 if d == 1 else QUART, QUART)
            i = 16 * h + (2 if d == 1 else 3)
            return remote(b, b, ss.at[i], rs.at[i], near(h, 1, d), z)

        def s2(h, d, o):
            b = block(buf, h, o, 0)
            i = 16 * h + 4 + 4 * (d == -1) + OFF.index(o)
            return remote(b, b, ss.at[i], rs.at[i], near(h, 2, d), z)

        def s2f(h, d, o):
            b = block(buf, h, o, -d)
            i = 16 * h + 12 + 2 * (d == -1) + FSET[d].index(o)
            return remote(b, b, ss.at[i], rs.at[i], near(h, 2, d), z)

        both = (0, 1)
        dirs = (1, -1)
        sent = []

        def go(copy):
            copy.start()
            sent.append(copy)

        def got1(h, d):
            b = block(buf, h, -d, 0)
            i = 16 * h + (0 if d == 1 else 1)
            remote(b, b, ss.at[i], rs.at[i], near(h, 1, d), z).wait_recv()

        def got1f(h, d):
            b = block(buf, h, 2, 0, 0 if d == 1 else QUART, QUART)
            i = 16 * h + (2 if d == 1 else 3)
            remote(b, b, ss.at[i], rs.at[i], near(h, 1, d), z).wait_recv()

        def got2(h, d, o):
            b = block(buf, h, o, -d)
            i = 16 * h + 4 + 4 * (d == -1) + OFF.index(o)
            remote(b, b, ss.at[i], rs.at[i], near(h, 2, d), z).wait_recv()

        def got2f(h, d, o):
            b = block(buf, h, o, 2)
            i = 16 * h + 12 + 2 * (d == -1) + FSET[d].index(o)
            remote(b, b, ss.at[i], rs.at[i], near(h, 2, d), z).wait_recv()

        for h in both:
            for d in dirs:
                go(s1(h, d))
        for h in both:
            for d in dirs:
                go(s2(h, d, 0))
        for d in dirs:
            for h in both:
                got1(h, d)
                go(s1f(h, d))
                go(s2(h, 1, -d))
                go(s2(h, -1, -d))
        for h in both:
            got2(h, -1, 0)
            go(s2f(h, -1, 0))
        for h in both:
            for d in dirs:
                got1f(h, d)
            for d in dirs:
                go(s2(h, d, 2))
        for h in both:
            got2(h, 1, 1)
            go(s2f(h, 1, 1))
            got2(h, -1, -1)
            go(s2f(h, -1, -1))
        for h in both:
            got2(h, 1, 2)
            go(s2f(h, 1, 2))
        for h in both:
            for d, o in ((1, 0), (1, -1), (-1, 1), (-1, 2)):
                got2(h, d, o)
            for d in dirs:
                for o in FSET[d]:
                    got2f(h, d, o)
        return sent

    def scatter(buf, ss, rs):
        both = (0, 1)
        dirs = (1, -1)
        sent = []

        def go(copy):
            copy.start()
            sent.append(copy)

        def slot_f(h, d, o):
            return 4 * h + 2 * (d == -1) + FSET[d].index(o)

        def slot_n(h, d, o):
            return 8 * h + 4 * (d == -1) + OFF.index(o)

        def slot_2(h, d):
            return 2 * h + (d == -1)

        def r1f(h, d, o):
            i = slot_f(h, d, o)
            return remote(block(buf, h, o, 2), rf.at[i], ss.at[i], rs.at[i], near(h, 2, d), z)

        def r1(h, d, o):
            i = slot_n(h, d, o)
            return remote(block(buf, h, o, d), rn.at[i], ss.at[8 + i], rs.at[8 + i], near(h, 2, d), z)

        def r2f(h, d):
            i = slot_2(h, d)
            b = block(buf, h, 2, 0, 0 if d == 1 else QUART, QUART)
            return remote(b, rf2.at[i], ss.at[24 + i], rs.at[24 + i], near(h, 1, d), z)

        def r2(h, d):
            i = slot_2(h, d)
            return remote(block(buf, h, d, 0), rn2.at[i], ss.at[28 + i], rs.at[28 + i], near(h, 1, d), z)

        for d, n in ((1, 0), (-1, 0), (1, 1), (-1, 1)):
            for h in both:
                go(r1f(h, d, FSET[d][n]))
        for h in both:
            go(r1(h, -1, 2))
            go(r1(h, 1, -1))
        for h in both:
            go(r1(h, -1, 1))
            go(r1(h, 1, 0))
        for d, n in ((1, 0), (-1, 0), (1, 1), (-1, 1)):
            for h in both:
                o = FSET[d][n]
                r1f(h, d, o).wait_recv()
                b = block(buf, h, o, d)
                b[...] = (b[...].astype(F32) + rf[slot_f(h, d, o)].astype(F32)).astype(BF16)
                go(r1(h, d, o))

        def total(h, o):
            r1(h, 1, o).wait_recv()
            r1(h, -1, o).wait_recv()
            b = block(buf, h, o, 0)
            return b[...].astype(F32) + rn[slot_n(h, 1, o)].astype(F32) + rn[slot_n(h, -1, o)].astype(F32)

        for h in both:
            block(buf, h, 2, 0)[...] = total(h, 2).astype(BF16)
            go(r2f(h, 1))
            go(r2f(h, -1))
        for h in both:
            for d in dirs:
                block(buf, h, d, 0)[...] = total(h, d).astype(BF16)
        for h in both:
            for d in dirs:
                r2f(h, d).wait_recv()
                b = block(buf, h, d, 0, 0 if d == 1 else QUART, QUART)
                b[...] = (b[...].astype(F32) + rf2[slot_2(h, d)].astype(F32)).astype(BF16)
                go(r2(h, d))
        for h in both:
            mid = total(h, 0)
            r2(h, 1).wait_recv()
            r2(h, -1).wait_recv()
            fb[pl.ds(h * HALF, HALF), :] = (
                mid + rn2[slot_2(h, 1)].astype(F32) + rn2[slot_2(h, -1)].astype(F32)
            ).astype(BF16)
        return sent

    def from_planes(copy_of):
        @loop(0, planes)
        def _(j):
            @pl.when(2 * j + c != z)
            def _():
                copy_of(j).wait_recv()

    def rz_got(j):
        return remote(
            route_ref.at[rows(p, ROWS), :], gr.at[x, y, :, lanes(j)], rz_s.at[0], rz_r.at[j], seq, z
        )

    from_planes(rz_got)

    @pl.when(owner)
    def _():
        own_r.wait()

    sent_r = gather(gr, ag_s, ag_r)

    own_x.wait()
    groups = min(4, nz)
    per = nz // groups
    depth = feats // groups

    def xs_copy(g, half):
        b = xt.at[pl.ds(g * depth, depth), lanes(half)]
        return remote(b, b, xs_s.at[g], xs_r.at[g], other, z)

    for g in range(groups):
        for i in range(per):
            frm = g * per + i

            @pl.when(frm != z)
            def _():
                remote(
                    tok_ref.at[:, lanes(z)], xt.at[pl.ds(frm * fz, fz), lanes(c)], tok_s.at[0], tok_r.at[frm], seq, z
                ).wait_recv()

        xs_copy(g, c).start()
    for g in range(groups):
        xs_copy(g, 1 - c).wait_recv()

    stok[...] = xt[...].T
    tile = min(256, width)

    @loop(0, width // tile)
    def _(j):
        at = pl.ds(pl.multiple_of(j * tile, tile), tile)
        part = gr[:, :, :, at].reshape(feats, tile)
        val = jnp.dot(stok[...], part, preferred_element_type=F32)
        lg[:, at] = val
        mrow = jnp.max(val, axis=0, keepdims=True)
        for t in range(tile // 128):
            mx[pl.ds(j * (tile // 128) + t, 1), :] = mrow[:, 128 * t : 128 * (t + 1)]

    if planes < 8:
        mx[planes:8, :] = jnp.zeros((8 - planes, 128), F32)

    def mx_copy(src, dst, ss, rs, k):
        return remote(src, dst.at[p], ss.at[k], rs.at[p], 2 * chip(k) + c, z)

    @loop(1, CHIPS)
    def _(k):
        mx_copy(mx, mxr, mx_s, mx_r, k).start()

    peak = jnp.max(lg[...], axis=1, keepdims=True)
    expo = jnp.exp(lg[...] - peak)
    cw[...] = expo.astype(BF16)
    tsum = jnp.sum(expo, axis=1, keepdims=True)
    peak_t = jnp.broadcast_to(peak, (2 * TOK, 128)).T
    tsum_t = jnp.broadcast_to(tsum, (2 * TOK, 128)).T
    trow[0:8, :] = peak_t[0:8, :]
    trow[8:16, :] = tsum_t[0:8, :]
    tr_copy = remote(trow, trow_r, tr_s.at[0], tr_r.at[0], other, z)
    tr_copy.start()

    def from_chips(dst, ss, rs):
        @loop(1, CHIPS)
        def _(k):
            remote(mx, dst.at[chip(k)], ss.at[0], rs.at[chip(k)], seq, z).wait_recv()

    mxr[p] = mx[...]
    from_chips(mxr, mx_s, mx_r)
    plane_peak = jnp.max(mxr[...], axis=0)
    for j in range(planes):
        prow[:, 128 * j : 128 * (j + 1)] = plane_peak[j : j + 1, :]

    expo = jnp.exp(lg[...] - prow[...])
    wt[...] = expo.astype(BF16)
    ssum = jnp.sum(expo, axis=0, keepdims=True)
    for j in range(planes):
        tt[j : j + 1, :] = ssum[:, 128 * j : 128 * (j + 1)]
    if planes < 8:
        tt[planes:8, :] = jnp.zeros((8 - planes, 128), F32)

    @loop(1, CHIPS)
    def _(k):
        mx_copy(tt, ttr, tt_s, tt_r, k).start()

    @loop(0, N)
    def _(i):
        part = xt[rows(i, feats // N), :]
        s[i] = jnp.dot(part, wt[...], preferred_element_type=F32).astype(BF16).reshape(N, ROWS, width)

    ttr[p] = tt[...]
    from_chips(ttr, tt_s, tt_r)
    plane_sum = jnp.sum(ttr[...], axis=0)
    for j in range(planes):
        zs[j, 0:1, :] = plane_peak[j : j + 1, :]
        zs[j, 1:2, :] = plane_sum[j : j + 1, :]
        zs[j, 2:8, :] = jnp.zeros((6, 128), F32)

    def zs_copy(j):
        return remote(zs.at[j], zst.at[z], zs_s.at[j], zs_r.at[z], seq, 2 * j + c)

    def to_planes(do):
        @loop(0, planes)
        def _(j):
            @pl.when(2 * j + c != z)
            def _():
                do(j)

    to_planes(lambda j: zs_copy(j).start())

    sent_s = scatter(s, rs_s, rs_r)

    def zb_copy(j):
        return remote(fb.at[:, lanes(j)], zb.at[z], zb_s.at[j], zb_r.at[z], seq, 2 * j + c)

    to_planes(lambda j: zb_copy(j).start())

    def si_copy(k, core, sem):
        return remote(si.at[p], si.at[p], sem, si_r.at[p], 2 * chip(k) + core, z)

    @pl.when(owner)
    def _():
        zst[z] = zs[z // 2]
        zb[z] = fb[:, pl.ds(mine, 128)]

        @loop(1, nz)
        def _(k):
            frm = zpeer(k)
            remote(zs.at[0], zst.at[frm], zs_s.at[0], zs_r.at[frm], seq, z).wait_recv()

        stat = zst[...]
        peaks = stat[:, 0:1, :]
        scale = jnp.exp(peaks - jnp.max(peaks, axis=0, keepdims=True))
        below = jnp.sum(scale * stat[:, 1:2, :], axis=0)

        @loop(1, nz)
        def _(k):
            frm = zpeer(k)
            remote(fb.at[:, lanes(0)], zb.at[frm], zb_s.at[0], zb_r.at[frm], seq, z).wait_recv()

        above = jnp.sum(scale * zb[...].astype(F32), axis=0)
        si[p] = (above / below).astype(BF16)

        @loop(1, CHIPS)
        def _(k):
            si_copy(k, c, si_s.at[k]).start()
            si_copy(k, 1 - c, si_s.at[CHIPS + k]).start()

        si_copy(0, 1 - c, si_s.at[CHIPS]).start()

    load_in.wait()
    load_out.wait()

    @loop(1, CHIPS)
    def _(k):
        remote(si.at[p], si.at[chip(k)], si_s.at[0], si_r.at[chip(k)], seq, z).wait_recv()

    @pl.when(jnp.logical_not(owner))
    def _():
        remote(si.at[p], si.at[p], si_s.at[0], si_r.at[p], seq, z).wait_recv()

    sp[...] = si[...].reshape(feats, 128).T
    experts = win.shape[0]
    each = 128 // experts

    @loop(0, experts)
    def _(e):
        h = jnp.dot(sp[rows(e, each), :], win[e], preferred_element_type=F32)
        h = jax.nn.gelu(h, approximate=True).astype(BF16)
        pacc[rows(e, each), :] = jnp.dot(h, wout[e], preferred_element_type=F32)

    pt[...] = pacc[...].T.astype(BF16).reshape(CHIPS, ROWS, 128)

    def pt_copy(k):
        return remote(pt.at[chip(k)], pb.at[seq], pt_s.at[k], pt_r.at[seq], 2 * chip(k) + oc, z)

    @loop(1, CHIPS)
    def _(k):
        pt_copy(k).start()

    @pl.when(jnp.logical_not(owner))
    def _():
        pt_copy(0).start()

    def ez_copy(k):
        b = ge.at[x, y, :, pl.ds(mine, 128)]
        return remote(b, b, ez_s.at[k], ez_r.at[z // 2], seq, zpeer(k))

    @pl.when(owner)
    def _():
        pb[seq] = pt[p]

        @loop(1, 2 * CHIPS)
        def _(k):
            frm = (seq + k) % (2 * CHIPS)
            remote(pt.at[0], pb.at[frm], pt_s.at[0], pt_r.at[frm], seq, z).wait_recv()

        ge[x, y, :, pl.ds(mine, 128)] = jnp.sum(pb[...].astype(F32), axis=0).astype(BF16)

        @loop(1, nz)
        def _(k):
            ez_copy(k).start()

    def ez_got(j):
        b = ge.at[x, y, :, lanes(j)]
        return remote(b, b, ez_s.at[0], ez_r.at[j], seq, z)

    from_planes(ez_got)
    sent_e = gather(ge, ae_s, ae_r)

    tr_copy.wait_recv()
    my = pl.multiple_of(c * TOK, TOK)
    their = pl.multiple_of((1 - c) * TOK, TOK)
    peak_a, peak_b = trow[0:1, pl.ds(my, TOK)], trow_r[0:1, pl.ds(my, TOK)]
    sum_a, sum_b = trow[8:9, pl.ds(my, TOK)], trow_r[8:9, pl.ds(my, TOK)]
    top = jnp.maximum(peak_a, peak_b)
    fac_a, fac_b = jnp.exp(peak_a - top), jnp.exp(peak_b - top)
    under = fac_a * sum_a + fac_b * sum_b
    fac_a, fac_b = fac_a / under, fac_b / under

    def os_copy(g):
        return remote(osend.at[g], orecv.at[g], os_s.at[g], os_r.at[g], other, z)

    def fin_copy(g, i):
        to = g * per + i
        return remote(ofin.at[to], out_ref.at[:, lanes(z)], fin_s.at[to], fin_r.at[z], seq, to)

    blocks = N // groups

    @loop(0, groups)
    def _(g):
        part = ge[pl.ds(g * blocks, blocks)].reshape(depth, width)
        both = lax.dot_general(part, cw[...], (((1,), (1,)), ((), ())), preferred_element_type=F32)
        first, second = both[:, :TOK], both[:, TOK:]
        oown[g] = jnp.where(c == 0, first, second)
        osend[g] = jnp.where(c == 0, second, first).astype(BF16)
        os_copy(g).start()

    own_o = pltpu.make_async_copy(ofin.at[z], out_ref.at[:, lanes(z)], own_s.at[2])

    @loop(0, groups)
    def _(g):
        os_copy(g).wait_recv()
        val = (oown[g] * fac_a + orecv[g].astype(F32) * fac_b).astype(BF16).reshape(per, fz, TOK)

        for i in range(per):
            to = g * per + i
            ofin[to] = val[i]

            @pl.when(to != z)
            def _():
                fin_copy(g, i).start()

            @pl.when(to == z)
            def _():
                own_o.start()

    own_o.wait()

    @loop(1, nz)
    def _(k):
        to = zpeer(k)
        remote(ofin.at[to], out_ref.at[:, lanes(to)], fin_s.at[to], fin_r.at[to], seq, z).wait()

    @loop(1, nz)
    def _(k):
        tok_copy(k).wait_send()

    @pl.when(owner)
    def _():
        @loop(1, nz)
        def _(k):
            rz_copy(k).wait_send()
            ez_copy(k).wait_send()

        @loop(1, CHIPS)
        def _(k):
            si_copy(k, c, si_s.at[k]).wait_send()
            si_copy(k, 1 - c, si_s.at[CHIPS + k]).wait_send()

        si_copy(0, 1 - c, si_s.at[CHIPS]).wait_send()

    @loop(1, CHIPS)
    def _(k):
        mx_copy(mx, mxr, mx_s, mx_r, k).wait_send()
        mx_copy(tt, ttr, tt_s, tt_r, k).wait_send()
        pt_copy(k).wait_send()

    @pl.when(jnp.logical_not(owner))
    def _():
        pt_copy(0).wait_send()

    to_planes(lambda j: zs_copy(j).wait_send())
    to_planes(lambda j: zb_copy(j).wait_send())
    tr_copy.wait_send()
    for g in range(groups):
        xs_copy(g, c).wait_send()
        os_copy(g).wait_send()
    for copy in sent_r + sent_s + sent_e:
        copy.wait_send()


def shards(nz, tokens, routing, w_in, w_out):
    tokens_t = tokens.T
    fz = tokens_t.shape[0]
    feats = fz * nz
    planes = nz // 2
    width = 128 * planes
    groups = min(4, nz)
    depth = feats // groups
    v, dma = pltpu.VMEM, pltpu.SemaphoreType.DMA
    scratch = [
        v((feats, 2 * TOK), BF16),
        v((N, N, ROWS, width), BF16),
        v((N, N, ROWS, width), BF16),
        v((2 * TOK, width), F32),
        v((2 * TOK, width), BF16),
        v((2 * TOK, width), BF16),
        v((2 * TOK, feats), BF16),
        v((N, N, ROWS, width), BF16),
        v((8, HALF, width), BF16),
        v((16, HALF, width), BF16),
        v((4, HALF // 2, width), BF16),
        v((4, HALF, width), BF16),
        v((ROWS, width), BF16),
        v((8, 128), F32),
        v((CHIPS, 8, 128), F32),
        v((8, 128), F32),
        v((CHIPS, 8, 128), F32),
        v((planes, 8, 128), F32),
        v((nz, 8, 128), F32),
        v((nz, ROWS, 128), BF16),
        v((CHIPS, ROWS, 128), BF16),
        v((128, feats), BF16),
        v((128, feats), F32),
        v((CHIPS, ROWS, 128), BF16),
        v((2 * CHIPS, ROWS, 128), BF16),
        v((groups, depth, TOK), BF16),
        v((groups, depth, TOK), BF16),
        v((groups, depth, TOK), F32),
        v((nz, fz, TOK), BF16),
        v((16, 2 * TOK), F32),
        v((16, 2 * TOK), F32),
        v((1, width), F32),
        v(w_in.shape, BF16),
        v(w_out.shape, BF16),
    ]
    counts = [
        nz, nz, groups, groups, nz, planes, 32, 32, 32, 32, 32, 32, CHIPS, CHIPS, CHIPS, CHIPS, planes, nz,
        planes, nz, 2 * CHIPS, CHIPS, CHIPS, 2 * CHIPS, nz, planes, groups, groups, nz, nz, 1, 1, 2, 3,
    ]
    scratch += [dma((n,)) for n in counts]
    out = pl.pallas_call(
        functools.partial(kernel, nz),
        out_shape=jax.ShapeDtypeStruct(tokens_t.shape, BF16),
        in_specs=[pl.BlockSpec(memory_space=pl.ANY)] * 4,
        out_specs=pl.BlockSpec(memory_space=pl.ANY),
        scratch_shapes=scratch,
        compiler_params=pltpu.CompilerParams(
            collective_id=0, has_side_effects=True, vmem_limit_bytes=56 * 1024 * 1024
        ),
    )(tokens_t, routing, w_in, w_out)
    return out.T


def solution(mesh):
    in_specs = (P("seq", "exp"), P(None, "exp"), P("exp", None, "seq"), P("exp", "seq", None))
    out_specs = P("seq", "exp")
    step = functools.partial(shards, mesh.shape["exp"])
    return jax.shard_map(step, mesh=mesh, in_specs=in_specs, out_specs=out_specs, check_vma=False)
```

time: 545 us -> 149 us (0.27)
  the two profiles are of different devices: /device:TPU:30 before, /device:TPU:448 now
where the time goes in v1:
time: 149 us; the launch traced here: 148 us
  Pallas kernels  147 us (99%)
  local copies, waits for them, and re-layouts  1.67 us (1%)
    pallas_call x1, Pallas kernels, shards(): pl.pallas_call(functools.partial(kernel, nz), out_shape=jax.ShapeDtypeStr...  147 us

profile of v1, /device:TPU:448, one launch (start us, length us, event | category | flops | bytes accessed | tf_op | source)
XLA Modules:
  0.0 148.4 jit_solution(11710491480747452106)
XLA Ops:
  0.0 146.7 %shard_map.46 = bf16[64,2048]{1,0:T(8,128)(2,1)} custom-call(bf16[64,2048]{1,0:T(8,128)(2,1)} %bitcast.3, bf16[1024,128]{1,0:T(8,128)(2,1)} %route_ref.1, bf16[8,1024,128]{2,1,0:T(8,128)(2,1)} %win_ref.1, bf16[8,128,1024]{2,1,0:T(8,128)(2,1)} %wout_ref.1), custom_call_target="tpu_custom_call" | custom-call | tf_op jit(solution)/shard_map/pallas_call | solution.py:663
  146.7 1.7 %copy.6 = bf16[2048,64]{0,1:T(8,128)(2,1)} copy(bf16[2048,64]{0,1:T(8,128)(2,1)} %bitcast.2) | data formatting | bytes 524288

commit v2 on v1

v2 whole, which is shorter than its diff:
```python
import functools

import jax
import jax.numpy as jnp
from jax import lax
from jax.experimental import pallas as pl
from jax.experimental.pallas import tpu as pltpu
from jax.sharding import PartitionSpec as P

MESH = pl.DeviceIdType.MESH
F32, BF16 = jnp.float32, jnp.bfloat16
N = 4
CHIPS = N * N
ROWS = 64
HALF = ROWS // 2
TOK = 128
FSET = {1: (2, 1), -1: (-1, 0)}
FAR = [(2, 2), (2, 1), (2, 3), (1, 2), (3, 2), (1, 1), (3, 3), (1, 3), (3, 1), (2, 0), (0, 2), (1, 0), (3, 0), (0, 1), (0, 3)]


def spot(f):
    return f % N, (f // N - f % N) % N


def remote(src, dst, send, recv, seq, z):
    return pltpu.make_async_remote_copy(
        src_ref=src, dst_ref=dst, send_sem=send, recv_sem=recv, device_id=(seq, z), device_id_type=MESH
    )


def kernel(nz, tok_ref, route_ref, win_ref, wout_ref, out_ref, *scratch):
    (
        xt, gr, ge, lg, wt, cw, stok, s, rf, rn, rf2, rn2, fb, st, stp, facs, zs, zst, zb, si, sp, pacc,
        pt, pb, osend, orecv, oown, ofin, trow, trow_r, win, wout,
        tok_s, tok_r, xs_s, xs_r, rz_s, rz_r, ag_s, ag_r, ae_s, ae_r, rs_s, rs_r, st_s, st_r, zs_s, zs_r,
        zb_s, zb_r, si_s, si_r, pt_s, pt_r, ez_s, ez_r, os_s, os_r, fin_s, fin_r, tr_s, tr_r, w_s, own_s, own_o_s,
    ) = scratch
    seq, z = lax.axis_index("seq"), lax.axis_index("exp")
    x, y, c = seq // (2 * N), (seq // 2) % N, seq % 2
    p = seq // 2
    planes = nz // 2
    width = 128 * planes
    feats = xt.shape[0]
    fz = feats // nz
    owner = c == z % 2
    oc = z % 2
    mine = pl.multiple_of((z // 2) * 128, 128)
    other = 2 * p + 1 - c

    def zpeer(k):
        m = k // 2
        return (z + nz // 2 + m * (2 * (k % 2) - 1) + nz) % nz

    def owned(cx, cy):
        return N * ((cx + cy) % N) + cx

    def off_chip(dx, dy):
        return (x + dx) % N, (y + dy) % N

    def owned_by(q):
        return owned(q // N, q % N)

    mf = owned(x, y)

    def chip(k):
        return (p + k) % CHIPS

    def lanes(j):
        return pl.ds(pl.multiple_of(j * 128, 128), 128)

    def rows(i, n):
        return pl.ds(pl.multiple_of(i * n, n), n)

    def loop(lo, hi):
        def run(body):
            def step(i, carry):
                body(i)
                return carry
            lax.fori_loop(lo, hi, step, 0)
        return run

    ends = []

    def finish():
        for end in ends:
            end()

    barrier = pltpu.get_barrier_semaphore()

    @loop(1, nz)
    def _(k):
        pl.semaphore_signal(barrier, inc=1, device_id=(seq, zpeer(k)), device_id_type=MESH)

    @loop(1, CHIPS)
    def _(k):
        pl.semaphore_signal(barrier, inc=1, device_id=(2 * chip(k) + c, z), device_id_type=MESH)
        pl.semaphore_signal(barrier, inc=1, device_id=(2 * chip(k) + 1 - c, z), device_id_type=MESH)

    pl.semaphore_signal(barrier, inc=1, device_id=(other, z), device_id_type=MESH)

    own_x = pltpu.make_async_copy(tok_ref.at[:, lanes(z)], xt.at[rows(z, fz), lanes(c)], own_s.at[0])
    own_x.start()
    own_r = pltpu.make_async_copy(route_ref.at[rows(mf, ROWS), :], gr.at[x, y, :, pl.ds(mine, 128)], own_s.at[1])

    @pl.when(owner)
    def _():
        own_r.start()

    load_in = pltpu.make_async_copy(win_ref, win, w_s.at[0])
    load_out = pltpu.make_async_copy(wout_ref, wout, w_s.at[1])

    pl.semaphore_wait(barrier, nz - 1 + 2 * (CHIPS - 1) + 1)

    def rz_copy(k):
        return remote(
            route_ref.at[rows(mf, ROWS), :], gr.at[x, y, :, pl.ds(mine, 128)], rz_s.at[k], rz_r.at[z // 2], seq, zpeer(k)
        )

    @pl.when(owner)
    def _():
        @loop(1, nz)
        def _(k):
            rz_copy(k).start()

    def rz_end():
        @pl.when(owner)
        def _():
            @loop(1, nz)
            def _(k):
                rz_copy(k).wait_send()

    ends.append(rz_end)

    def tok_copy(k):
        to = zpeer(k)
        return remote(
            tok_ref.at[:, lanes(to)], xt.at[rows(z, fz), lanes(c)], tok_s.at[k], tok_r.at[z], seq, to
        )


    load_in.start()
    load_out.start()

    def near(h, axis, d):
        along_x = (axis == 1) == (h == 0)
        nx = (x + d) % N if along_x else x
        ny = y if along_x else (y + d) % N
        return 2 * (N * nx + ny) + c

    def place(h, o1, o2):
        return ((x + o1) % N, (y + o2) % N) if h == 0 else ((x + o2) % N, (y + o1) % N)

    def block(buf, h, o1, o2, lo=0, n=HALF):
        bx, by = place(h, o1, o2)
        return buf.at[bx, by, pl.ds(h * HALF + lo, n), :]

    OFF = (0, 1, -1, 2)
    QUART = HALF // 2

    def gather(buf, ss, rs, first=None, middle=None, second=None, third=None):
        def s1(h, d):
            b = block(buf, h, 0, 0)
            i = 16 * h + (0 if d == 1 else 1)
            return remote(b, b, ss.at[i], rs.at[i], near(h, 1, d), z)

        def s1f(h, d):
            b = block(buf, h, -d, 0, 0 if d == 1 else QUART, QUART)
            i = 16 * h + (2 if d == 1 else 3)
            return remote(b, b, ss.at[i], rs.at[i], near(h, 1, d), z)

        def s2(h, d, o):
            b = block(buf, h, o, 0)
            i = 16 * h + 4 + 4 * (d == -1) + OFF.index(o)
            return remote(b, b, ss.at[i], rs.at[i], near(h, 2, d), z)

        def s2f(h, d, o):
            b = block(buf, h, o, -d)
            i = 16 * h + 12 + 2 * (d == -1) + FSET[d].index(o)
            return remote(b, b, ss.at[i], rs.at[i], near(h, 2, d), z)

        both = (0, 1)
        dirs = (1, -1)

        def go(copy):
            copy.start()
            ends.append(copy.wait_send)

        def got1(h, d):
            b = block(buf, h, -d, 0)
            i = 16 * h + (0 if d == 1 else 1)
            remote(b, b, ss.at[i], rs.at[i], near(h, 1, d), z).wait_recv()

        def got1f(h, d):
            b = block(buf, h, 2, 0, 0 if d == 1 else QUART, QUART)
            i = 16 * h + (2 if d == 1 else 3)
            remote(b, b, ss.at[i], rs.at[i], near(h, 1, d), z).wait_recv()

        def got2(h, d, o):
            b = block(buf, h, o, -d)
            i = 16 * h + 4 + 4 * (d == -1) + OFF.index(o)
            remote(b, b, ss.at[i], rs.at[i], near(h, 2, d), z).wait_recv()

        def got2f(h, d, o):
            b = block(buf, h, o, 2)
            i = 16 * h + 12 + 2 * (d == -1) + FSET[d].index(o)
            remote(b, b, ss.at[i], rs.at[i], near(h, 2, d), z).wait_recv()

        for h in both:
            for d in dirs:
                go(s1(h, d))
        for h in both:
            for d in dirs:
                go(s2(h, d, 0))
        for d in dirs:
            for h in both:
                got1(h, d)
                go(s1f(h, d))
                go(s2(h, 1, -d))
                go(s2(h, -1, -d))
        for h in both:
            got2(h, -1, 0)
            go(s2f(h, -1, 0))
        for h in both:
            for d in dirs:
                got1f(h, d)
            for d in dirs:
                go(s2(h, d, 2))
        if first:
            first()
        for h in both:
            got2(h, 1, 1)
            go(s2f(h, 1, 1))
            got2(h, -1, -1)
            go(s2f(h, -1, -1))
        if middle:
            middle()
        for h in both:
            for d, o in ((1, 0), (1, -1), (-1, 1)):
                got2(h, d, o)
        if second:
            second()
        for h in both:
            got2(h, 1, 2)
            go(s2f(h, 1, 2))
        if third:
            third()
        for h in both:
            got2(h, -1, 2)
            for d in dirs:
                for o in FSET[d]:
                    got2f(h, d, o)

    def scatter(buf, ss, rs, started, summed):
        both = (0, 1)
        dirs = (1, -1)

        def go(copy):
            copy.start()
            ends.append(copy.wait_send)

        def slot_f(h, d, o):
            return 4 * h + 2 * (d == -1) + FSET[d].index(o)

        def slot_n(h, d, o):
            return 8 * h + 4 * (d == -1) + OFF.index(o)

        def slot_2(h, d):
            return 2 * h + (d == -1)

        def r1f(h, d, o):
            i = slot_f(h, d, o)
            return remote(block(buf, h, o, 2), rf.at[i], ss.at[i], rs.at[i], near(h, 2, d), z)

        def r1(h, d, o):
            i = slot_n(h, d, o)
            return remote(block(buf, h, o, d), rn.at[i], ss.at[8 + i], rs.at[8 + i], near(h, 2, d), z)

        def r2f(h, d):
            i = slot_2(h, d)
            b = block(buf, h, 2, 0, 0 if d == 1 else QUART, QUART)
            return remote(b, rf2.at[i], ss.at[24 + i], rs.at[24 + i], near(h, 1, d), z)

        def r2(h, d):
            i = slot_2(h, d)
            return remote(block(buf, h, d, 0), rn2.at[i], ss.at[28 + i], rs.at[28 + i], near(h, 1, d), z)

        for d, n in ((1, 0), (-1, 0), (1, 1), (-1, 1)):
            for h in both:
                go(r1f(h, d, FSET[d][n]))
        for h in both:
            go(r1(h, -1, 2))
            go(r1(h, 1, -1))
        for h in both:
            go(r1(h, -1, 1))
            go(r1(h, 1, 0))
        started()

        def scaled(val, i):
            return val.astype(F32) * facs[i : i + 1, :]

        def sender(h, d):
            return (3 if h == 0 else 1) + (d == 1)

        for d, n in ((1, 0), (-1, 0), (1, 1), (-1, 1)):
            for h in both:
                o = FSET[d][n]
                r1f(h, d, o).wait_recv()
                b = block(buf, h, o, d)
                b[...] = (scaled(b[...], 0) + scaled(rf[slot_f(h, d, o)], sender(h, d))).astype(BF16)
                go(r1(h, d, o))

        def total(h, o):
            val = scaled(block(buf, h, o, 0)[...], 0)
            for d in dirs:
                r1(h, d, o).wait_recv()
                part = rn[slot_n(h, d, o)]
                val += part.astype(F32) if o in FSET[d] else scaled(part, sender(h, d))
            return val

        for h in both:
            block(buf, h, 2, 0)[...] = total(h, 2).astype(BF16)
            go(r2f(h, 1))
            go(r2f(h, -1))
        summed()
        for h in both:
            for d in dirs:
                block(buf, h, d, 0)[...] = total(h, d).astype(BF16)
        for h in both:
            for d in dirs:
                r2f(h, d).wait_recv()
                b = block(buf, h, d, 0, 0 if d == 1 else QUART, QUART)
                b[...] = (b[...].astype(F32) + rf2[slot_2(h, d)].astype(F32)).astype(BF16)
                go(r2(h, d))
        for h in both:
            mid = total(h, 0)
            r2(h, 1).wait_recv()
            r2(h, -1).wait_recv()
            fb[pl.ds(h * HALF, HALF), :] = (
                mid + rn2[slot_2(h, 1)].astype(F32) + rn2[slot_2(h, -1)].astype(F32)
            ).astype(BF16)

    def from_planes(copy_of):
        @loop(0, planes)
        def _(j):
            @pl.when(2 * j + c != z)
            def _():
                copy_of(j).wait_recv()

    def rz_got(j):
        return remote(
            route_ref.at[rows(mf, ROWS), :], gr.at[x, y, :, lanes(j)], rz_s.at[0], rz_r.at[j], seq, z
        )

    from_planes(rz_got)

    @loop(1, nz)
    def _(k):
        tok_copy(k).start()

    def tok_end():
        @loop(1, nz)
        def _(k):
            tok_copy(k).wait_send()

    ends.append(tok_end)

    @pl.when(owner)
    def _():
        own_r.wait()

    groups = min(4, nz)
    per = nz // groups
    depth = feats // groups

    def xs_copy(g, half):
        b = xt.at[pl.ds(g * depth, depth), lanes(half)]
        return remote(b, b, xs_s.at[g], xs_r.at[g], other, z)

    def swap():
        for g in range(groups):
            for i in range(per):
                frm = g * per + i

                @pl.when(frm != z)
                def _():
                    remote(
                        tok_ref.at[:, lanes(z)], xt.at[pl.ds(frm * fz, fz), lanes(c)], tok_s.at[0], tok_r.at[frm], seq, z
                    ).wait_recv()

            xs_copy(g, c).start()
            ends.append(xs_copy(g, c).wait_send)

    own_x.wait()
    gather(gr, ag_s, ag_r, third=swap)
    for g in range(groups):
        xs_copy(g, 1 - c).wait_recv()

    stok[...] = xt[...].T
    tile = min(256, width)

    @loop(0, width // tile)
    def _(j):
        at = pl.ds(pl.multiple_of(j * tile, tile), tile)
        part = jnp.concatenate([gr[spot(f) + (slice(None), at)] for f in range(CHIPS)], axis=0)
        val = jnp.dot(stok[...], part, preferred_element_type=F32)
        lg[:, at] = val
        peak = jnp.max(val, axis=0, keepdims=True)
        expo = jnp.exp(val - peak)
        wt[:, at] = expo.astype(BF16)
        tot = jnp.sum(expo, axis=0, keepdims=True)
        for t in range(tile // 128):
            st[pl.ds(j * (tile // 128) + t, 1), :] = peak[:, 128 * t : 128 * (t + 1)]
            st[pl.ds(8 + j * (tile // 128) + t, 1), :] = tot[:, 128 * t : 128 * (t + 1)]

    if planes < 8:
        st[planes:8, :] = jnp.zeros((8 - planes, 128), F32)
        st[8 + planes : 16, :] = jnp.zeros((8 - planes, 128), F32)

    def st_copy(i):
        cx, cy = off_chip(*FAR[i])
        return remote(st, stp.at[p], st_s.at[i], st_r.at[p], 2 * (N * cx + cy) + c, z)

    for i in range(CHIPS - 1):
        st_copy(i).start()
        ends.append(st_copy(i).wait_send)
    stp[p] = st[...]

    for i in range(N):
        part = jnp.dot(xt[i * N * ROWS : (i + 1) * N * ROWS, :], wt[...], preferred_element_type=F32)
        for k in range(N):
            s[spot(N * i + k)] = part[k * ROWS : (k + 1) * ROWS, :].astype(BF16)

    def softmax():
        peak = jnp.max(lg[...], axis=1, keepdims=True)
        expo = jnp.exp(lg[...] - peak)
        cw[...] = expo.astype(BF16)
        tsum = jnp.sum(expo, axis=1, keepdims=True)
        peak_t = jnp.broadcast_to(peak, (2 * TOK, 128)).T
        tsum_t = jnp.broadcast_to(tsum, (2 * TOK, 128)).T
        trow[0:8, :] = peak_t[0:8, :]
        trow[8:16, :] = tsum_t[0:8, :]
        tr_copy.start()

    tr_copy = remote(trow, trow_r, tr_s.at[0], tr_r.at[0], other, z)
    ends.append(tr_copy.wait_send)

    def factors():
        @loop(1, CHIPS)
        def _(k):
            remote(st, stp.at[chip(k)], st_s.at[0], st_r.at[chip(k)], seq, z).wait_recv()

        high = jnp.max(stp[:, 0:8, :], axis=0)
        for i, (dx, dy) in enumerate(((0, 0), (1, 0), (-1, 0), (0, 1), (0, -1))):
            cx, cy = off_chip(dx, dy)
            fac = jnp.exp(stp[N * cx + cy, 0:8, :] - high)
            for j in range(planes):
                facs[i : i + 1, 128 * j : 128 * (j + 1)] = fac[j : j + 1, :]

    def totals():
        high = jnp.max(stp[:, 0:8, :], axis=0)
        tot = jnp.sum(jnp.exp(stp[:, 0:8, :] - high) * stp[:, 8:16, :], axis=0)
        for j in range(planes):
            zs[j, 0:1, :] = high[j : j + 1, :]
            zs[j, 1:2, :] = tot[j : j + 1, :]
            zs[j, 2:8, :] = jnp.zeros((6, 128), F32)
        to_planes(lambda j: zs_copy(j).start())

    def zs_copy(j):
        return remote(zs.at[j], zst.at[z], zs_s.at[j], zs_r.at[z], seq, 2 * j + c)

    def to_planes(do):
        @loop(1, nz)
        def _(k):
            to = zpeer(k)

            @pl.when(to % 2 == c)
            def _():
                do(to // 2)

    ends.append(lambda: to_planes(lambda j: zs_copy(j).wait_send()))

    def zs_got():
        @loop(1, nz)
        def _(k):
            frm = zpeer(k)
            remote(zs.at[0], zst.at[frm], zs_s.at[0], zs_r.at[frm], seq, z).wait_recv()

    scatter(s, rs_s, rs_r, factors, totals)

    def zb_copy(j):
        return remote(fb.at[:, lanes(j)], zb.at[z], zb_s.at[j], zb_r.at[z], seq, 2 * j + c)

    to_planes(lambda j: zb_copy(j).start())
    ends.append(lambda: to_planes(lambda j: zb_copy(j).wait_send()))
    softmax()

    def si_copy(dx, dy, core, sem):
        cx, cy = off_chip(dx, dy)
        return remote(si.at[mf], si.at[mf], sem, si_r.at[mf], 2 * (N * cx + cy) + core, z)

    si_all = [si_copy(dx, dy, core, si_s.at[2 * i + t]) for i, (dx, dy) in enumerate(FAR) for t, core in enumerate((c, 1 - c))]
    si_all.append(si_copy(0, 0, 1 - c, si_s.at[2 * CHIPS - 2]))

    @pl.when(owner)
    def _():
        zst[z] = zs[z // 2]
        zb[z] = fb[:, pl.ds(mine, 128)]

        zs_got()
        stat = zst[...]
        peaks = stat[:, 0:1, :]
        scale = jnp.exp(peaks - jnp.max(peaks, axis=0, keepdims=True))
        below = jnp.sum(scale * stat[:, 1:2, :], axis=0)

        @loop(1, nz)
        def _(k):
            frm = zpeer(k)
            remote(fb.at[:, lanes(0)], zb.at[frm], zb_s.at[0], zb_r.at[frm], seq, z).wait_recv()

        above = jnp.sum(scale * zb[...].astype(F32), axis=0)
        si[mf] = (above / below).astype(BF16)
        for copy in si_all:
            copy.start()

    def si_end():
        @pl.when(owner)
        def _():
            for copy in si_all:
                copy.wait_send()

    ends.append(si_end)

    @loop(1, CHIPS)
    def _(k):
        f = owned_by(chip(k))
        remote(si.at[f], si.at[f], si_s.at[0], si_r.at[f], seq, z).wait_recv()

    @pl.when(jnp.logical_not(owner))
    def _():
        remote(si.at[mf], si.at[mf], si_s.at[0], si_r.at[mf], seq, z).wait_recv()

    load_in.wait()
    load_out.wait()
    sp[...] = si[...].reshape(feats, 128).T
    experts = win.shape[0]
    each = 128 // experts

    @loop(0, experts)
    def _(e):
        h = jnp.dot(sp[rows(e, each), :], win[e], preferred_element_type=F32)
        h = jax.nn.gelu(h, approximate=True).astype(BF16)
        pacc[rows(e, each), :] = jnp.dot(h, wout[e], preferred_element_type=F32)

    pt[...] = pacc[...].T.astype(BF16).reshape(CHIPS, ROWS, 128)

    def pt_copy(dx, dy, i):
        cx, cy = off_chip(dx, dy)
        return remote(pt.at[owned(cx, cy)], pb.at[seq], pt_s.at[i], pt_r.at[seq], 2 * (N * cx + cy) + oc, z)

    for i, (dx, dy) in enumerate(FAR):
        pt_copy(dx, dy, i).start()
        ends.append(pt_copy(dx, dy, i).wait_send)
    pt_near = pt_copy(0, 0, CHIPS - 1)

    @pl.when(jnp.logical_not(owner))
    def _():
        pt_near.start()

    def pt_end():
        @pl.when(jnp.logical_not(owner))
        def _():
            pt_near.wait_send()

    ends.append(pt_end)

    def ez_copy(k):
        b = ge.at[x, y, :, pl.ds(mine, 128)]
        return remote(b, b, ez_s.at[k], ez_r.at[z // 2], seq, zpeer(k))

    @pl.when(owner)
    def _():
        pb[seq] = pt[mf]

        @loop(1, 2 * CHIPS)
        def _(k):
            frm = (seq + k) % (2 * CHIPS)
            remote(pt.at[0], pb.at[frm], pt_s.at[0], pt_r.at[frm], seq, z).wait_recv()

        ge[x, y, :, pl.ds(mine, 128)] = jnp.sum(pb[...].astype(F32), axis=0).astype(BF16)

        @loop(1, nz)
        def _(k):
            ez_copy(k).start()

    def ez_end():
        @pl.when(owner)
        def _():
            @loop(1, nz)
            def _(k):
                ez_copy(k).wait_send()

    ends.append(ez_end)

    def ez_got(j):
        b = ge.at[x, y, :, lanes(j)]
        return remote(b, b, ez_s.at[0], ez_r.at[j], seq, z)

    from_planes(ez_got)
    tr_copy.wait_recv()
    my = pl.multiple_of(c * TOK, TOK)
    peak_a, peak_b = trow[0:1, pl.ds(my, TOK)], trow_r[0:1, pl.ds(my, TOK)]
    sum_a, sum_b = trow[8:9, pl.ds(my, TOK)], trow_r[8:9, pl.ds(my, TOK)]
    top = jnp.maximum(peak_a, peak_b)
    fac_a, fac_b = jnp.exp(peak_a - top), jnp.exp(peak_b - top)
    under = fac_a * sum_a + fac_b * sum_b
    fac_a, fac_b = fac_a / under, fac_b / under

    pieces = [
        [(h, o1, 0) for h in (0, 1) for o1 in OFF],
        [(h, o1, o2) for h in (0, 1) for o1 in OFF[:3] for o2 in (1, -1)],
        [(h, o1, 2) for h in (0, 1) for o1 in OFF] + [(h, 2, o2) for h in (0, 1) for o2 in (1, -1)],
    ]
    starts = (0, 8, 20)
    each = CHIPS // nz

    def os_copy(g):
        part = pl.ds(starts[g], len(pieces[g]))
        return remote(osend.at[part], orecv.at[part], os_s.at[g], os_r.at[g], other, z)

    def mix(g):
        n = len(pieces[g])
        part = jnp.concatenate([block(ge, *piece)[...] for piece in pieces[g]], axis=0)
        val = lax.dot_general(part, cw[...], (((1,), (1,)), ((), ())), preferred_element_type=F32)
        first, second = val[:, :TOK], val[:, TOK:]
        at = pl.ds(starts[g], n)
        oown[at] = jnp.where(c == 0, first, second).reshape(n, HALF, TOK)
        osend[at] = jnp.where(c == 0, second, first).astype(BF16).reshape(n, HALF, TOK)
        os_copy(g).start()
        ends.append(os_copy(g).wait_send)

    def fin_copy(q, h, f):
        to = f // each
        at = out_ref.at[pl.ds(pl.multiple_of((f % each) * ROWS + h * HALF, HALF), HALF), lanes(z)]
        return remote(ofin.at[q], at, fin_s.at[q], fin_r.at[z, (f % each) * 2 + h], seq, to)

    def own_o(q, h, f):
        at = out_ref.at[pl.ds(pl.multiple_of((f % each) * ROWS + h * HALF, HALF), HALF), lanes(z)]
        return pltpu.make_async_copy(ofin.at[q], at, own_o_s.at[(f % each) * 2 + h])

    def send(g):
        os_copy(g).wait_recv()
        n = len(pieces[g])
        at = pl.ds(starts[g], n)
        ofin[at] = (oown[at] * fac_a + orecv[at].astype(F32) * fac_b).astype(BF16)
        for i, (h, o1, o2) in enumerate(pieces[g]):
            q = starts[g] + i
            f = owned(*place(h, o1, o2))

            @pl.when(f // each != z)
            def _():
                fin_copy(q, h, f).start()

            @pl.when(f // each == z)
            def _():
                own_o(q, h, f).start()

    gather(ge, ae_s, ae_r, first=lambda: mix(0), middle=lambda: send(0), second=lambda: mix(1), third=lambda: send(1))
    mix(2)
    send(2)

    @loop(0, 2 * each)
    def _(i):
        at = out_ref.at[pl.ds(pl.multiple_of(i * HALF, HALF), HALF), lanes(z)]
        pltpu.make_async_copy(ofin.at[0], at, own_o_s.at[i]).wait()

    @loop(1, nz)
    def _(k):
        frm = zpeer(k)
        for i in range(2 * each):
            at = out_ref.at[pl.ds(i * HALF, HALF), lanes(frm)]
            remote(ofin.at[0], at, fin_s.at[0], fin_r.at[frm, i], seq, z).wait_recv()

    for g in range(3):
        for i, (h, o1, o2) in enumerate(pieces[g]):
            f = owned(*place(h, o1, o2))

            @pl.when(f // each != z)
            def _():
                fin_copy(starts[g] + i, h, f).wait_send()

    finish()


def shards(nz, tokens, routing, w_in, w_out):
    tokens_t = tokens.T
    fz = tokens_t.shape[0]
    feats = fz * nz
    planes = nz // 2
    width = 128 * planes
    groups = min(4, nz)
    v, dma = pltpu.VMEM, pltpu.SemaphoreType.DMA
    scratch = [
        v((feats, 2 * TOK), BF16),
        v((N, N, ROWS, width), BF16),
        v((N, N, ROWS, width), BF16),
        v((2 * TOK, width), F32),
        v((2 * TOK, width), BF16),
        v((2 * TOK, width), BF16),
        v((2 * TOK, feats), BF16),
        v((N, N, ROWS, width), BF16),
        v((8, HALF, width), BF16),
        v((16, HALF, width), BF16),
        v((4, HALF // 2, width), BF16),
        v((4, HALF, width), BF16),
        v((ROWS, width), BF16),
        v((16, 128), F32),
        v((CHIPS, 16, 128), F32),
        v((8, width), F32),
        v((planes, 8, 128), F32),
        v((nz, 8, 128), F32),
        v((nz, ROWS, 128), BF16),
        v((CHIPS, ROWS, 128), BF16),
        v((128, feats), BF16),
        v((128, feats), F32),
        v((CHIPS, ROWS, 128), BF16),
        v((2 * CHIPS, ROWS, 128), BF16),
        v((2 * CHIPS, HALF, TOK), BF16),
        v((2 * CHIPS, HALF, TOK), BF16),
        v((2 * CHIPS, HALF, TOK), F32),
        v((2 * CHIPS, HALF, TOK), BF16),
        v((16, 2 * TOK), F32),
        v((16, 2 * TOK), F32),
        v(w_in.shape, BF16),
        v(w_out.shape, BF16),
    ]
    counts = [
        nz, nz, groups, groups, nz, planes, 32, 32, 32, 32, 32, 32, CHIPS, CHIPS, planes, nz,
        planes, nz, 2 * CHIPS, CHIPS, CHIPS, 2 * CHIPS, nz, planes, 3, 3, 2 * CHIPS, (nz, 2 * CHIPS // nz), 1, 1, 2, 3,
        2 * CHIPS // nz,
    ]
    scratch += [dma(n if isinstance(n, tuple) else (n,)) for n in counts]
    out = pl.pallas_call(
        functools.partial(kernel, nz),
        out_shape=jax.ShapeDtypeStruct(tokens_t.shape, BF16),
        in_specs=[pl.BlockSpec(memory_space=pl.ANY)] * 4,
        out_specs=pl.BlockSpec(memory_space=pl.ANY),
        scratch_shapes=scratch,
        compiler_params=pltpu.CompilerParams(
            collective_id=0, has_side_effects=True, vmem_limit_bytes=56 * 1024 * 1024
        ),
    )(tokens_t, routing, w_in, w_out)
    return out.T


def solution(mesh):
    in_specs = (P("seq", "exp"), P(None, "exp"), P("exp", None, "seq"), P("exp", "seq", None))
    out_specs = P("seq", "exp")
    step = functools.partial(shards, mesh.shape["exp"])
    return jax.shard_map(step, mesh=mesh, in_specs=in_specs, out_specs=out_specs, check_vma=False)
```

time: 149 us -> 129 us (0.87)
  the two profiles are of different devices: /device:TPU:448 before, /device:TPU:18 now
where the time goes in v2:
time: 129 us
  Pallas kernels  127 us (98%)
  local copies, waits for them, and re-layouts  1.67 us (1%)
    pallas_call x1, Pallas kernels, shards(): pl.pallas_call(functools.partial(kernel, nz), out_shape=jax.ShapeDtypeStr...  127 us

profile of v2, /device:TPU:18, one launch (start us, length us, event | category | flops | bytes accessed | tf_op | source)
XLA Modules:
  0.0 128.8 jit_solution(3572190390511106154)
XLA Ops:
  0.0 127.2 %shard_map.46 = bf16[64,2048]{1,0:T(8,128)(2,1)} custom-call(bf16[64,2048]{1,0:T(8,128)(2,1)} %bitcast.3, bf16[1024,128]{1,0:T(8,128)(2,1)} %route_ref.1, bf16[8,1024,128]{2,1,0:T(8,128)(2,1)} %win_ref.1, bf16[8,128,1024]{2,1,0:T(8,128)(2,1)} %wout_ref.1), custom_call_target="tpu_custom_call" | custom-call | tf_op jit(solution)/shard_map/pallas_call | solution.py:742
  127.2 1.7 %copy.6 = bf16[2048,64]{0,1:T(8,128)(2,1)} copy(bf16[2048,64]{0,1:T(8,128)(2,1)} %bitcast.2) | data formatting | bytes 524288

commit v3 on v2

--- a/solution.py
+++ b/solution.py
@@ -30,8 +30,8 @@
 
 def kernel(nz, tok_ref, route_ref, win_ref, wout_ref, out_ref, *scratch):
     (
-        xt, gr, ge, lg, wt, cw, stok, s, rf, rn, rf2, rn2, fb, st, stp, facs, zs, zst, zb, si, sp, pacc,
-        pt, pb, osend, orecv, oown, ofin, trow, trow_r, win, wout,
+        xt, gr, ge, lg, wt, cw, stok, s, rf, rn, rn2, fb, st, stp, facs, zs, zst, zb, si, sp, pacc,
+        pt, pb, osend, orecv, oown, ofin, trow, trow_r, rv, tv, win, wout,
         tok_s, tok_r, xs_s, xs_r, rz_s, rz_r, ag_s, ag_r, ae_s, ae_r, rs_s, rs_r, st_s, st_r, zs_s, zs_r,
         zb_s, zb_r, si_s, si_r, pt_s, pt_r, ez_s, ez_r, os_s, os_r, fin_s, fin_r, tr_s, tr_r, w_s, own_s, own_o_s,
     ) = scratch
@@ -98,8 +98,6 @@
 
     pl.semaphore_signal(barrier, inc=1, device_id=(other, z), device_id_type=MESH)
 
-    own_x = pltpu.make_async_copy(tok_ref.at[:, lanes(z)], xt.at[rows(z, fz), lanes(c)], own_s.at[0])
-    own_x.start()
     own_r = pltpu.make_async_copy(route_ref.at[rows(mf, ROWS), :], gr.at[x, y, :, pl.ds(mine, 128)], own_s.at[1])
 
     @pl.when(owner)
@@ -108,12 +106,21 @@
 
     load_in = pltpu.make_async_copy(win_ref, win, w_s.at[0])
     load_out = pltpu.make_async_copy(wout_ref, wout, w_s.at[1])
+    stage_r = pltpu.make_async_copy(route_ref.at[rows(mf, ROWS), :], rv, own_s.at[2])
+    stage_t = pltpu.make_async_copy(tok_ref, tv, own_s.at[0])
+    stage_r.start()
+    stage_t.start()
+    load_in.start()
+    load_out.start()
+    stage_r.wait()
+    stage_t.wait()
+    xt[rows(z, fz), lanes(c)] = tv[:, lanes(z)]
 
     pl.semaphore_wait(barrier, nz - 1 + 2 * (CHIPS - 1) + 1)
 
     def rz_copy(k):
         return remote(
-            route_ref.at[rows(mf, ROWS), :], gr.at[x, y, :, pl.ds(mine, 128)], rz_s.at[k], rz_r.at[z // 2], seq, zpeer(k)
+            rv, gr.at[x, y, :, pl.ds(mine, 128)], rz_s.at[k], rz_r.at[z // 2], seq, zpeer(k)
         )
 
     @pl.when(owner)
@@ -134,12 +141,9 @@
     def tok_copy(k):
         to = zpeer(k)
         return remote(
-            tok_ref.at[:, lanes(to)], xt.at[rows(z, fz), lanes(c)], tok_s.at[k], tok_r.at[z], seq, to
+            tv.at[:, lanes(to)], xt.at[rows(z, fz), lanes(c)], tok_s.at[k], tok_r.at[z], seq, to
         )
 
-
-    load_in.start()
-    load_out.start()
 
     def near(h, axis, d):
         along_x = (axis == 1) == (h == 0)
@@ -155,17 +159,12 @@
         return buf.at[bx, by, pl.ds(h * HALF + lo, n), :]
 
     OFF = (0, 1, -1, 2)
-    QUART = HALF // 2
-
-    def gather(buf, ss, rs, first=None, middle=None, second=None, third=None):
+    ONE = (1, -1, 2)
+
+    def gather(buf, ss, rs, first=None, middle=None, second=None, third=None, fourth=None):
         def s1(h, d):
             b = block(buf, h, 0, 0)
-            i = 16 * h + (0 if d == 1 else 1)
-            return remote(b, b, ss.at[i], rs.at[i], near(h, 1, d), z)
-
-        def s1f(h, d):
-            b = block(buf, h, -d, 0, 0 if d == 1 else QUART, QUART)
-            i = 16 * h + (2 if d == 1 else 3)
+            i = 16 * h + ONE.index(d)
             return remote(b, b, ss.at[i], rs.at[i], near(h, 1, d), z)
 
         def s2(h, d, o):
@@ -187,12 +186,7 @@
 
         def got1(h, d):
             b = block(buf, h, -d, 0)
-            i = 16 * h + (0 if d == 1 else 1)
-            remote(b, b, ss.at[i], rs.at[i], near(h, 1, d), z).wait_recv()
-
-        def got1f(h, d):
-            b = block(buf, h, 2, 0, 0 if d == 1 else QUART, QUART)
-            i = 16 * h + (2 if d == 1 else 3)
+            i = 16 * h + ONE.index(d)
             remote(b, b, ss.at[i], rs.at[i], near(h, 1, d), z).wait_recv()
 
         def got2(h, d, o):
@@ -206,7 +200,7 @@
             remote(b, b, ss.at[i], rs.at[i], near(h, 2, d), z).wait_recv()
 
         for h in both:
-            for d in dirs:
+            for d in (2, 1, -1):
                 go(s1(h, d))
         for h in both:
             for d in dirs:
@@ -214,15 +208,13 @@
         for d in dirs:
             for h in both:
                 got1(h, d)
-                go(s1f(h, d))
                 go(s2(h, 1, -d))
                 go(s2(h, -1, -d))
         for h in both:
             got2(h, -1, 0)
             go(s2f(h, -1, 0))
         for h in both:
-            for d in dirs:
-                got1f(h, d)
+            got1(h, 2)
             for d in dirs:
                 go(s2(h, d, 2))
         if first:
@@ -245,10 +237,13 @@
         if third:
             third()
         for h in both:
+            for d, o in ((1, 1), (-1, -1), (-1, 0)):
+                got2f(h, d, o)
+        if fourth:
+            fourth()
+        for h in both:
             got2(h, -1, 2)
-            for d in dirs:
-                for o in FSET[d]:
-                    got2f(h, d, o)
+            got2f(h, 1, 2)
 
     def scatter(buf, ss, rs, started, summed):
         both = (0, 1)
@@ -265,7 +260,7 @@
             return 8 * h + 4 * (d == -1) + OFF.index(o)
 
         def slot_2(h, d):
-            return 2 * h + (d == -1)
+            return 3 * h + ONE.index(d)
 
         def r1f(h, d, o):
             i = slot_f(h, d, o)
@@ -275,14 +270,9 @@
             i = slot_n(h, d, o)
             return remote(block(buf, h, o, d), rn.at[i], ss.at[8 + i], rs.at[8 + i], near(h, 2, d), z)
 
-        def r2f(h, d):
-            i = slot_2(h, d)
-            b = block(buf, h, 2, 0, 0 if d == 1 else QUART, QUART)
-            return remote(b, rf2.at[i], ss.at[24 + i], rs.at[24 + i], near(h, 1, d), z)
-
         def r2(h, d):
             i = slot_2(h, d)
-            return remote(block(buf, h, d, 0), rn2.at[i], ss.at[28 + i], rs.at[28 + i], near(h, 1, d), z)
+            return remote(block(buf, h, d, 0), rn2.at[i], ss.at[24 + i], rs.at[24 + i], near(h, 1, d), z)
 
         for d, n in ((1, 0), (-1, 0), (1, 1), (-1, 1)):
             for h in both:
@@ -319,25 +309,18 @@
 
         for h in both:
             block(buf, h, 2, 0)[...] = total(h, 2).astype(BF16)
-            go(r2f(h, 1))
-            go(r2f(h, -1))
+            go(r2(h, 2))
         summed()
         for h in both:
             for d in dirs:
                 block(buf, h, d, 0)[...] = total(h, d).astype(BF16)
-        for h in both:
-            for d in dirs:
-                r2f(h, d).wait_recv()
-                b = block(buf, h, d, 0, 0 if d == 1 else QUART, QUART)
-                b[...] = (b[...].astype(F32) + rf2[slot_2(h, d)].astype(F32)).astype(BF16)
                 go(r2(h, d))
         for h in both:
-            mid = total(h, 0)
-            r2(h, 1).wait_recv()
-            r2(h, -1).wait_recv()
-            fb[pl.ds(h * HALF, HALF), :] = (
-                mid + rn2[slot_2(h, 1)].astype(F32) + rn2[slot_2(h, -1)].astype(F32)
-            ).astype(BF16)
+            val = total(h, 0)
+            for d in ONE:
+                r2(h, d).wait_recv()
+                val += rn2[slot_2(h, d)].astype(F32)
+            fb[pl.ds(h * HALF, HALF), :] = val.astype(BF16)
 
     def from_planes(copy_of):
         @loop(0, planes)
@@ -348,7 +331,7 @@
 
     def rz_got(j):
         return remote(
-            route_ref.at[rows(mf, ROWS), :], gr.at[x, y, :, lanes(j)], rz_s.at[0], rz_r.at[j], seq, z
+            rv, gr.at[x, y, :, lanes(j)], rz_s.at[0], rz_r.at[j], seq, z
         )
 
     from_planes(rz_got)
@@ -384,13 +367,12 @@
                 @pl.when(frm != z)
                 def _():
                     remote(
-                        tok_ref.at[:, lanes(z)], xt.at[pl.ds(frm * fz, fz), lanes(c)], tok_s.at[0], tok_r.at[frm], seq, z
+                        tv.at[:, lanes(z)], xt.at[pl.ds(frm * fz, fz), lanes(c)], tok_s.at[0], tok_r.at[frm], seq, z
                     ).wait_recv()
 
             xs_copy(g, c).start()
             ends.append(xs_copy(g, c).wait_send)
 
-    own_x.wait()
     gather(gr, ag_s, ag_r, third=swap)
     for g in range(groups):
         xs_copy(g, 1 - c).wait_recv()
@@ -618,9 +600,10 @@
     pieces = [
         [(h, o1, 0) for h in (0, 1) for o1 in OFF],
         [(h, o1, o2) for h in (0, 1) for o1 in OFF[:3] for o2 in (1, -1)],
-        [(h, o1, 2) for h in (0, 1) for o1 in OFF] + [(h, 2, o2) for h in (0, 1) for o2 in (1, -1)],
+        [(h, o1, 2) for h in (0, 1) for o1 in OFF[:3]],
+        [(h, 2, o2) for h in (0, 1) for o2 in (1, -1, 2)],
     ]
-    starts = (0, 8, 20)
+    starts = (0, 8, 20, 26)
     each = CHIPS // nz
 
     def os_copy(g):
@@ -664,10 +647,12 @@
             def _():
                 own_o(q, h, f).start()
 
-    gather(ge, ae_s, ae_r, first=lambda: mix(0), middle=lambda: send(0), second=lambda: mix(1), third=lambda: send(1))
-    mix(2)
+    gather(ge, ae_s, ae_r, first=lambda: mix(0), middle=lambda: send(0), second=lambda: mix(1), third=lambda: send(1), fourth=lambda: mix(2))
+    mix(3)
     send(2)
-
+    send(3)
+
+    finish()
     @loop(0, 2 * each)
     def _(i):
         at = out_ref.at[pl.ds(pl.multiple_of(i * HALF, HALF), HALF), lanes(z)]
@@ -680,15 +665,13 @@
             at = out_ref.at[pl.ds(i * HALF, HALF), lanes(frm)]
             remote(ofin.at[0], at, fin_s.at[0], fin_r.at[frm, i], seq, z).wait_recv()
 
-    for g in range(3):
+    for g in range(4):
         for i, (h, o1, o2) in enumerate(pieces[g]):
             f = owned(*place(h, o1, o2))
 
             @pl.when(f // each != z)
             def _():
                 fin_copy(starts[g] + i, h, f).wait_send()
-
-    finish()
 
 
 def shards(nz, tokens, routing, w_in, w_out):
@@ -710,8 +693,7 @@
         v((N, N, ROWS, width), BF16),
         v((8, HALF, width), BF16),
         v((16, HALF, width), BF16),
-        v((4, HALF // 2, width), BF16),
-        v((4, HALF, width), BF16),
+        v((6, HALF, width), BF16),
         v((ROWS, width), BF16),
         v((16, 128), F32),
         v((CHIPS, 16, 128), F32),
@@ -730,12 +712,14 @@
         v((2 * CHIPS, HALF, TOK), BF16),
         v((16, 2 * TOK), F32),
         v((16, 2 * TOK), F32),
+        v((ROWS, 128), BF16),
+        v(tokens_t.shape, BF16),
         v(w_in.shape, BF16),
         v(w_out.shape, BF16),
     ]
     counts = [
         nz, nz, groups, groups, nz, planes, 32, 32, 32, 32, 32, 32, CHIPS, CHIPS, planes, nz,
-        planes, nz, 2 * CHIPS, CHIPS, CHIPS, 2 * CHIPS, nz, planes, 3, 3, 2 * CHIPS, (nz, 2 * CHIPS // nz), 1, 1, 2, 3,
+        planes, nz, 2 * CHIPS, CHIPS, CHIPS, 2 * CHIPS, nz, planes, 4, 4, 2 * CHIPS, (nz, 2 * CHIPS // nz), 1, 1, 2, 3,
         2 * CHIPS // nz,
     ]
     scratch += [dma(n if isinstance(n, tuple) else (n,)) for n in counts]

time: 129 us -> 123 us (0.953)
  Pallas kernels: 127 us -> 121 us
    pallas_call x1, Pallas kernels: 127 us -> 121 us  [shards(): pl.pallas_call(functools.partial(kernel, nz), out_shape=jax.ShapeDtypeStr...]
where the time goes in v3:
time: 123 us
  Pallas kernels  121 us (98%)
  local copies, waits for them, and re-layouts  1.67 us (1%)
    pallas_call x1, Pallas kernels, shards(): pl.pallas_call(functools.partial(kernel, nz), out_shape=jax.ShapeDtypeStr...  121 us

profile of v3, /device:TPU:18, one launch (start us, length us, event | category | flops | bytes accessed | tf_op | source)
XLA Modules:
  0.0 123.1 jit_solution(220779519701851865)
XLA Ops:
  0.0 121.4 %shard_map.46 = bf16[64,2048]{1,0:T(8,128)(2,1)} custom-call(bf16[64,2048]{1,0:T(8,128)(2,1)} %bitcast.3, bf16[1024,128]{1,0:T(8,128)(2,1)} %route_ref.1, bf16[8,1024,128]{2,1,0:T(8,128)(2,1)} %win_ref.1, bf16[8,128,1024]{2,1,0:T(8,128)(2,1)} %wout_ref.1), custom_call_target="tpu_custom_call" | custom-call | tf_op jit(solution)/shard_map/pallas_call | solution.py:726
  121.4 1.7 %copy.6 = bf16[2048,64]{0,1:T(8,128)(2,1)} copy(bf16[2048,64]{0,1:T(8,128)(2,1)} %bitcast.2) | data formatting | bytes 524288

commit v4 on v3

--- a/solution.py
+++ b/solution.py
@@ -334,11 +334,19 @@
             rv, gr.at[x, y, :, lanes(j)], rz_s.at[0], rz_r.at[j], seq, z
         )
 
+    @pl.when(owner)
+    def _():
+        @loop(1, nz)
+        def _(k):
+            tok_copy(k).start()
+
     from_planes(rz_got)
 
-    @loop(1, nz)
-    def _(k):
-        tok_copy(k).start()
+    @pl.when(jnp.logical_not(owner))
+    def _():
+        @loop(1, nz)
+        def _(k):
+            tok_copy(k).start()
 
     def tok_end():
         @loop(1, nz)
@@ -480,8 +488,7 @@
         cx, cy = off_chip(dx, dy)
         return remote(si.at[mf], si.at[mf], sem, si_r.at[mf], 2 * (N * cx + cy) + core, z)
 
-    si_all = [si_copy(dx, dy, core, si_s.at[2 * i + t]) for i, (dx, dy) in enumerate(FAR) for t, core in enumerate((c, 1 - c))]
-    si_all.append(si_copy(0, 0, 1 - c, si_s.at[2 * CHIPS - 2]))
+    si_near = si_copy(0, 0, 1 - c, si_s.at[2 * CHIPS - 2])
 
     @pl.when(owner)
     def _():
@@ -501,25 +508,27 @@
 
         above = jnp.sum(scale * zb[...].astype(F32), axis=0)
         si[mf] = (above / below).astype(BF16)
-        for copy in si_all:
-            copy.start()
+        si_near.start()
+
+    @pl.when(jnp.logical_not(owner))
+    def _():
+        si_near.wait_recv()
 
     def si_end():
         @pl.when(owner)
         def _():
-            for copy in si_all:
-                copy.wait_send()
+            si_near.wait_send()
 
     ends.append(si_end)
+
+    for i, (dx, dy) in enumerate(FAR):
+        si_copy(dx, dy, c, si_s.at[i]).start()
+        ends.append(si_copy(dx, dy, c, si_s.at[i]).wait_send)
 
     @loop(1, CHIPS)
     def _(k):
         f = owned_by(chip(k))
         remote(si.at[f], si.at[f], si_s.at[0], si_r.at[f], seq, z).wait_recv()
-
-    @pl.when(jnp.logical_not(owner))
-    def _():
-        remote(si.at[mf], si.at[mf], si_s.at[0], si_r.at[mf], seq, z).wait_recv()
 
     load_in.wait()
     load_out.wait()

time: 123 us -> 122 us (level)
  the two profiles are of different devices: /device:TPU:18 before, /device:TPU:23 now
where the time goes in v4:
time: 122 us
  Pallas kernels  120 us (98%)
  local copies, waits for them, and re-layouts  1.67 us (1%)
    pallas_call x1, Pallas kernels, shards(): pl.pallas_call(functools.partial(kernel, nz), out_shape=jax.ShapeDtypeStr...  120 us

profile of v4, /device:TPU:23, one launch (start us, length us, event | category | flops | bytes accessed | tf_op | source)
XLA Modules:
  0.0 121.7 jit_solution(14788574776157730357)
XLA Ops:
  0.0 120.0 %shard_map.46 = bf16[64,2048]{1,0:T(8,128)(2,1)} custom-call(bf16[64,2048]{1,0:T(8,128)(2,1)} %bitcast.3, bf16[1024,128]{1,0:T(8,128)(2,1)} %route_ref.1, bf16[8,1024,128]{2,1,0:T(8,128)(2,1)} %win_ref.1, bf16[8,128,1024]{2,1,0:T(8,128)(2,1)} %wout_ref.1), custom_call_target="tpu_custom_call" | custom-call | tf_op jit(solution)/shard_map/pallas_call | solution.py:735
  120.0 1.7 %copy.6 = bf16[2048,64]{0,1:T(8,128)(2,1)} copy(bf16[2048,64]{0,1:T(8,128)(2,1)} %bitcast.2) | data formatting | bytes 524288

commit v5 on v4

--- a/solution.py
+++ b/solution.py
@@ -274,9 +274,17 @@
             i = slot_2(h, d)
             return remote(block(buf, h, d, 0), rn2.at[i], ss.at[24 + i], rs.at[24 + i], near(h, 1, d), z)
 
-        for d, n in ((1, 0), (-1, 0), (1, 1), (-1, 1)):
-            for h in both:
-                go(r1f(h, d, FSET[d][n]))
+        weighted(2)
+        for d in dirs:
+            for o in FSET[d]:
+                go(r1f(1, d, o))
+        go(r1f(0, 1, 2))
+        weighted(1)
+        go(r1f(0, 1, 1))
+        weighted(-1)
+        go(r1f(0, -1, -1))
+        weighted(0)
+        go(r1f(0, -1, 0))
         for h in both:
             go(r1(h, -1, 2))
             go(r1(h, 1, -1))
@@ -415,10 +423,12 @@
         ends.append(st_copy(i).wait_send)
     stp[p] = st[...]
 
-    for i in range(N):
-        part = jnp.dot(xt[i * N * ROWS : (i + 1) * N * ROWS, :], wt[...], preferred_element_type=F32)
+    def weighted(o):
+        bx = (x + o) % N
+        part = jnp.concatenate([xt[rows(owned(bx, k), ROWS), :] for k in range(N)], axis=0)
+        val = jnp.dot(part, wt[...], preferred_element_type=F32).astype(BF16)
         for k in range(N):
-            s[spot(N * i + k)] = part[k * ROWS : (k + 1) * ROWS, :].astype(BF16)
+            s[bx, k] = val[k * ROWS : (k + 1) * ROWS, :]
 
     def softmax():
         peak = jnp.max(lg[...], axis=1, keepdims=True)

time: 122 us -> 122 us (level)
  the two profiles are of different devices: /device:TPU:23 before, /device:TPU:18 now
where the time goes in v5:
time: 122 us
  Pallas kernels  120 us (98%)
  local copies, waits for them, and re-layouts  1.67 us (1%)
    pallas_call x1, Pallas kernels, shards(): pl.pallas_call(functools.partial(kernel, nz), out_shape=jax.ShapeDtypeStr...  120 us

profile of v5, /device:TPU:18, one launch (start us, length us, event | category | flops | bytes accessed | tf_op | source)
XLA Modules:
  0.0 121.5 jit_solution(1438783988729452676)
XLA Ops:
  0.0 119.9 %shard_map.46 = bf16[64,2048]{1,0:T(8,128)(2,1)} custom-call(bf16[64,2048]{1,0:T(8,128)(2,1)} %bitcast.3, bf16[1024,128]{1,0:T(8,128)(2,1)} %route_ref.1, bf16[8,1024,128]{2,1,0:T(8,128)(2,1)} %win_ref.1, bf16[8,128,1024]{2,1,0:T(8,128)(2,1)} %wout_ref.1), custom_call_target="tpu_custom_call" | custom-call | tf_op jit(solution)/shard_map/pallas_call | solution.py:745
  119.9 1.7 %copy.6 = bf16[2048,64]{0,1:T(8,128)(2,1)} copy(bf16[2048,64]{0,1:T(8,128)(2,1)} %bitcast.2) | data formatting | bytes 524288
